TPU v7x, 32 devices: a whole 2x2x4 slice. The times are simulated.
32 devices in a mesh: rep: 8 (over y, x, core), shard: 4 (over z).
Axes of the slice: x: 2, y: 2, z: 4, core: 2. Of those that a mesh axis runs over, the one named last changes fastest.
Arguments:
- activations: bfloat16 [4096, 4096], P(('rep', 'shard')), may hold values from -6 to 6
- cotangent: bfloat16 [4096, 896], P(('rep', 'shard')), may hold values from -0.099609375 to 0.099609375
- weight: bfloat16 [8, 4096, 896], P('rep', 'shard'), may hold values from -6 to 6
- momentum: bfloat16 [8, 4096, 896], P('rep', 'shard'), may hold values from -6 to 6
- step_index: int32 [1], replicated, may hold values from 0 to 999
Outputs:
- averaged: bfloat16 [8, 4096, 896], P('rep', 'shard')
- momentum_new: bfloat16 [8, 4096, 896], P('rep', 'shard')
All inputs are finite; a program needn't handle non-finite values.
Results may differ from a plain program's by a relative error of at most 0.012.
Values may be sent and summed in bfloat16 or wider, within the bound.
A program may use at most 64 MiB of HBM per device.

v0:
```python
import functools

import jax
import jax.numpy as jnp
from jax import lax
from jax.experimental import pallas as pl
from jax.experimental.pallas import tpu as pltpu
from jax.sharding import PartitionSpec as P

MESH = pl.DeviceIdType.MESH
STEP = 128


def cuts(size, step):
    step = step if size % step == 0 else size
    return [(at, step) for at in range(0, size, step)]


def plan(rows, cols):
    a_chunks, c_chunks = cuts(rows, STEP), cuts(cols, STEP)
    order = sorted(
        [((i + 1) / len(c_chunks), 0, "c", i) for i in range(len(c_chunks))]
        + [((i + 1) / len(a_chunks), 1, "a", i) for i in range(len(a_chunks))]
    )
    events, rows_in, cols_in = [], 0, 0
    for _, _, kind, i in order:
        if kind == "a":
            at, size = a_chunks[i]
            block = (at, size, 0, cols_in)
            rows_in = at + size
        else:
            at, size = c_chunks[i]
            block = (0, rows_in, at, size)
            cols_in = at + size
        events.append((kind, i, at, size, block if block[1] and block[3] else None))
    return events


def kernel(
    n_rep,
    n_shard,
    by,
    act,
    cot,
    weight,
    momentum,
    avg_out,
    mom_out,
    act_all,
    cot_all,
    w_in,
    m_in,
    m_new,
    half,
    other,
    avg,
    load_sem,
    act_send,
    act_recv,
    cot_send,
    cot_recv,
    rep_send,
    rep_recv,
    mom_sem,
    avg_sem,
):
    rep, shard = lax.axis_index("rep"), lax.axis_index("shard")
    tok = cot.shape[0]
    rows, cols = weight.shape
    events = plan(rows, cols)
    ahead = lax.rem(rep + by, n_rep)
    behind = lax.rem(rep + (n_rep - by), n_rep)

    mine = pl.ds(pl.multiple_of(shard * tok, tok), tok)
    loads = [
        pltpu.make_async_copy(
            act.at[:, pl.ds(pl.multiple_of(shard * rows, rows), rows)], act_all.at[mine, :], load_sem.at[0]
        ),
        pltpu.make_async_copy(cot, cot_all.at[mine, :], load_sem.at[1]),
        pltpu.make_async_copy(momentum, m_in, load_sem.at[2]),
        pltpu.make_async_copy(weight, w_in, load_sem.at[3]),
    ]
    for load in loads:
        load.start()

    barrier = pltpu.get_barrier_semaphore()
    for off in range(1, n_shard):
        pl.semaphore_signal(
            barrier, inc=1, device_id={"shard": lax.rem(shard + off, n_shard)}, device_id_type=MESH
        )
    for partner in (ahead, behind):
        pl.semaphore_signal(barrier, inc=1, device_id={"rep": partner}, device_id_type=MESH)
    pl.semaphore_wait(barrier, n_shard + 1)

    sends = {}

    def start(kind, i, at, size, _):
        if kind == "c":
            relay(i, at, size, 0)
            return
        for off in range(1, n_shard):
            to = lax.rem(shard + off, n_shard)
            copy = pltpu.make_async_remote_copy(
                src_ref=act.at[:, pl.ds(pl.multiple_of(to * rows + at, size), size)],
                dst_ref=act_all.at[mine, pl.ds(at, size)],
                send_sem=act_send.at[i, off - 1],
                recv_sem=act_recv.at[i, off - 1],
                device_id={"shard": to},
                device_id_type=MESH,
            )
            copy.start()
            sends[i, off] = copy

    def hop(i, at, size, side, far, come):
        way = 1 - 2 * side
        owner = shard - way * (far + come)
        slot = cot_all.at[pl.ds(pl.multiple_of(owner * tok, tok), tok), pl.ds(at, size)]
        return pltpu.make_async_remote_copy(
            src_ref=slot if far or come else cot.at[:, pl.ds(at, size)],
            dst_ref=slot,
            send_sem=cot_send.at[i, side, far],
            recv_sem=cot_recv.at[i, side, far],
            device_id={"shard": shard - way if come else shard + way},
            device_id_type=MESH,
        )

    def passes(side, far):
        if side == 0:
            return (shard >= far) & (shard + 1 < n_shard)
        return (shard + far < n_shard) & (shard >= 1)

    def comes(side, far):
        return shard >= far + 1 if side == 0 else shard + far + 1 < n_shard

    def relay(i, at, size, far):
        for side in range(2):
            if far:
                pl.when(comes(side, far - 1))(lambda side=side: hop(i, at, size, side, far - 1, 1).wait_recv())
            if far < last:
                pl.when(passes(side, far))(lambda side=side: hop(i, at, size, side, far, 0).start())

    last = n_shard - 1

    def turn(n):
        if 0 <= n + last < len(events):
            start(*events[n + last])
        for far in range(1, last):
            if 0 <= n + last - far < len(events):
                kind, i, at, size, _ = events[n + last - far]
                if kind == "c":
                    relay(i, at, size, far)

    for n in range(-last, 0):
        turn(n)

    for load in loads:
        load.wait()

    tile = STEP if rows % STEP == 0 else rows
    outs, reps, blocks = [], [], []
    for n, (kind, i, at, size, block) in enumerate(events):
        if kind == "c":
            relay(i, at, size, last)
        else:
            for off in range(1, n_shard):
                sends[i, off].wait_recv()
        turn(n)
        if block is None:
            continue
        r0, height, c0, width = block
        across = pl.ds(c0, width)

        def one(t, _):
            down = pl.ds(pl.multiple_of(r0 + t * tile, tile), tile)
            grad = lax.dot_general(
                act_all[:, down],
                cot_all[:, across],
                (((0,), (0,)), ((), ())),
                preferred_element_type=jnp.float32,
            )
            new = (0.9 * m_in[down, across].astype(jnp.float32) + grad).astype(jnp.bfloat16)
            m_new[down, across] = new
            half[down, across] = (
                w_in[down, across].astype(jnp.float32) - 0.5 * new.astype(jnp.float32)
            ).astype(jnp.bfloat16)
            return 0

        lax.fori_loop(0, height // tile, one, 0)
        e = len(blocks)
        here = (pl.ds(r0, height), across)
        copy = pltpu.make_async_remote_copy(
            src_ref=half.at[here],
            dst_ref=other.at[here],
            send_sem=rep_send.at[e],
            recv_sem=rep_recv.at[e],
            device_id={"rep": ahead},
            device_id_type=MESH,
        )
        copy.start()
        reps.append(copy)
        out = pltpu.make_async_copy(m_new.at[here], mom_out.at[here], mom_sem.at[e])
        out.start()
        outs.append(out)
        blocks.append(block)

    for e, (r0, height, c0, width) in enumerate(blocks):
        reps[e].wait_recv()
        across = pl.ds(c0, width)

        def mean(t, _):
            down = pl.ds(pl.multiple_of(r0 + t * tile, tile), tile)
            avg[down, across] = (
                0.5 * (half[down, across].astype(jnp.float32) + other[down, across].astype(jnp.float32))
            ).astype(jnp.bfloat16)
            return 0

        lax.fori_loop(0, height // tile, mean, 0)
        here = (pl.ds(r0, height), across)
        out = pltpu.make_async_copy(avg.at[here], avg_out.at[here], avg_sem.at[e])
        out.start()
        outs.append(out)

    for copy in sends.values():
        copy.wait_send()
    for kind, i, at, size, _ in events:
        if kind == "c":
            for far in range(last):
                for side in range(2):
                    pl.when(passes(side, far))(
                        lambda i=i, at=at, size=size, side=side, far=far: hop(i, at, size, side, far, 0).wait_send()
                    )
    for copy in reps:
        copy.wait_send()
    for out in outs:
        out.wait()


def fused(n_rep, n_shard, level, activations, cotangent, weight, momentum):
    tok, (rows, cols) = cotangent.shape[0], weight.shape
    events = plan(rows, cols)
    n_a = sum(kind == "a" for kind, *_ in events)
    n_c = len(events) - n_a
    n_b = sum(event[-1] is not None for event in events)
    dma = pltpu.SemaphoreType.DMA
    whole = pltpu.VMEM((rows, cols), jnp.bfloat16)
    shape = jax.ShapeDtypeStruct((rows, cols), jnp.bfloat16)
    anywhere = pl.BlockSpec(memory_space=pl.ANY)
    return pl.pallas_call(
        functools.partial(kernel, n_rep, n_shard, 1 << level),
        out_shape=(shape, shape),
        in_specs=[anywhere] * 4,
        out_specs=(anywhere, anywhere),
        scratch_shapes=[
            pltpu.VMEM((n_shard * tok, rows), jnp.bfloat16),
            pltpu.VMEM((n_shard * tok, cols), jnp.bfloat16),
            *[whole] * 6,
            dma((4,)),
            dma((n_a, n_shard - 1)),
            dma((n_a, n_shard - 1)),
            dma((n_c, 2, n_shard - 1)),
            dma((n_c, 2, n_shard - 1)),
            dma((n_b,)),
            dma((n_b,)),
            dma((n_b,)),
            dma((n_b,)),
        ],
        compiler_params=pltpu.CompilerParams(
            collective_id=level + 1, has_side_effects=True, vmem_limit_bytes=48 << 20
        ),
        cost_estimate=pl.CostEstimate(
            flops=2 * n_shard * tok * rows * cols, bytes_accessed=10 * rows * cols, transcendentals=0
        ),
    )(activations, cotangent, weight, momentum)


def per_device(activations, cotangent, weight, momentum, step_index):
    n_rep, n_shard = lax.axis_size("rep"), lax.axis_size("shard")
    levels = n_rep.bit_length() - 1
    branches = [functools.partial(fused, n_rep, n_shard, level) for level in range(levels)]
    averaged, momentum_new = lax.switch(
        step_index[0] % levels, branches, activations, cotangent, weight[0], momentum[0]
    )
    return averaged[None], momentum_new[None]


def solution(mesh):
    return jax.shard_map(
        per_device,
        mesh=mesh,
        in_specs=(
            P(("rep", "shard"), None),
            P(("rep", "shard"), None),
            P("rep", "shard", None),
            P("rep", "shard", None),
            P(),
        ),
        out_specs=(P("rep", "shard", None), P("rep", "shard", None)),
        check_vma=False,
    )
```

profile of v0, /device:TPU:0, one launch (start us, length us, event | category | flops | bytes accessed | tf_op | source)
XLA Modules:
  0.0 73.2 jit_solution(5267446231888041453)
XLA Ops:
  1.3 69.4 %conditional.1 = ((bf16[1024,896]{1,0:T(8,128)(2,1)S(1)}, bf16[1024,896]{1,0:T(8,128)(2,1)S(1)})) conditional(s32[]{:T(128)} %clamp.3, (bf16[128,4096]{1,0:T(8,128)(2,1)}, bf16[128,896]{1,0:T(8,128)(2,1)}, bf16[1024,896]{1,0:T(8,128)(2,1)}, bf16[1024,896]{1,0:T(8,128)(2,1)}) %tuple.41, (bf16[128,4096]{1,0:T(8,128)(2,1)}, ...), branch_computations={%region_0.1_spmd, %region_1.2_spmd, %region_2.3_spmd} | conditional | flops 939524096 | bytes 9175048 | solution.py:280
  1.3 69.0 %branch_1_fun.1 = (bf16[1024,896]{1,0:T(8,128)(2,1)S(1)}, bf16[1024,896]{1,0:T(8,128)(2,1)S(1)}) custom-call(bf16[128,4096]{1,0:T(8,128)(2,1)} %get-tuple-element.38.act, bf16[128,896]{1,0:T(8,128)(2,1)} %get-tuple-element.39.cot, bf16[1024,896]{1,0:T(8,128)(2,1)} %get-tuple-element.40.weight, bf16[1024,896]{1,0:T(8,128)(2,1)} %get-tuple-element.41.momentum), custom_call_target="tpu_custom_call" | custom-call | flops 939524096 | bytes 9175040 | tf_op jit(solution)/shard_map/cond/branch_1_fun/pallas_call | solution.py:248
  70.7 1.2 %copy.16 = bf16[1,1024,896]{2,1,0:T(8,128)(2,1)} copy(bf16[1,1024,896]{2,1,0:T(8,128)(2,1)S(1)} %bitcast.11) | data formatting | bytes 3670016
  72.0 1.2 %copy.17 = bf16[1,1024,896]{2,1,0:T(8,128)(2,1)} copy(bf16[1,1024,896]{2,1,0:T(8,128)(2,1)S(1)} %bitcast.12) | data formatting | bytes 3670016
where the time goes:
time: 73.4 us; the launch traced here: 73.2 us
  Pallas kernels  69 us (94%)
  local copies, waits for them, and re-layouts  2.46 us (3%)
  between operations  1.3 us (2%)
    pallas_call x1, Pallas kernels, fused(): pl.pallas_call(functools.partial(kernel, n_rep, n_shard, 1 << level), out...  69 us
    unnamed x2, local copies, waits for them, and re-layouts  2.46 us

commit v1 on v0

--- a/solution.py
+++ b/solution.py
@@ -1,4 +1,5 @@
 import functools
+import math
 
 import jax
 import jax.numpy as jnp
@@ -11,16 +12,31 @@
 STEP = 128
 
 
-def cuts(size, step):
-    step = step if size % step == 0 else size
-    return [(at, step) for at in range(0, size, step)]
+def cuts(size, step=STEP):
+    if size % step:
+        return [(0, size)]
+    chunks, at = [(0, step)], step
+    while at < size:
+        width = min(2 * step, size - at)
+        chunks.append((at, width))
+        at += width
+    return chunks
+
+
+def tiles(block, step=2 * STEP):
+    r0, height, c0, width = block
+    return [
+        (pl.ds(r, min(step, r0 + height - r)), pl.ds(c, min(step, c0 + width - c)))
+        for r in range(r0, r0 + height, step)
+        for c in range(c0, c0 + width, step)
+    ]
 
 
 def plan(rows, cols):
-    a_chunks, c_chunks = cuts(rows, STEP), cuts(cols, STEP)
+    a_chunks, c_chunks = cuts(rows), cuts(cols)
     order = sorted(
-        [((i + 1) / len(c_chunks), 0, "c", i) for i in range(len(c_chunks))]
-        + [((i + 1) / len(a_chunks), 1, "a", i) for i in range(len(a_chunks))]
+        [((at + size) / cols, 0, "c", i) for i, (at, size) in enumerate(c_chunks)]
+        + [((at + size) / rows, 1, "a", i) for i, (at, size) in enumerate(a_chunks)]
     )
     events, rows_in, cols_in = [], 0, 0
     for _, _, kind, i in order:
@@ -47,6 +63,7 @@
     avg_out,
     mom_out,
     act_all,
+    act_t,
     cot_all,
     w_in,
     m_in,
@@ -101,7 +118,7 @@
         for off in range(1, n_shard):
             to = lax.rem(shard + off, n_shard)
             copy = pltpu.make_async_remote_copy(
-                src_ref=act.at[:, pl.ds(pl.multiple_of(to * rows + at, size), size)],
+                src_ref=act.at[:, pl.ds(pl.multiple_of(to * rows + at, math.gcd(rows, at)), size)],
                 dst_ref=act_all.at[mine, pl.ds(at, size)],
                 send_sem=act_send.at[i, off - 1],
                 recv_sem=act_recv.at[i, off - 1],
@@ -156,7 +173,6 @@
     for load in loads:
         load.wait()
 
-    tile = STEP if rows % STEP == 0 else rows
     outs, reps, blocks = [], [], []
     for n, (kind, i, at, size, block) in enumerate(events):
         if kind == "c":
@@ -165,29 +181,18 @@
             for off in range(1, n_shard):
                 sends[i, off].wait_recv()
         turn(n)
+        if kind == "a":
+            act_t[pl.ds(at, size), :] = act_all[:, pl.ds(at, size)].T
         if block is None:
             continue
         r0, height, c0, width = block
-        across = pl.ds(c0, width)
-
-        def one(t, _):
-            down = pl.ds(pl.multiple_of(r0 + t * tile, tile), tile)
-            grad = lax.dot_general(
-                act_all[:, down],
-                cot_all[:, across],
-                (((0,), (0,)), ((), ())),
-                preferred_element_type=jnp.float32,
-            )
-            new = (0.9 * m_in[down, across].astype(jnp.float32) + grad).astype(jnp.bfloat16)
-            m_new[down, across] = new
-            half[down, across] = (
-                w_in[down, across].astype(jnp.float32) - 0.5 * new.astype(jnp.float32)
-            ).astype(jnp.bfloat16)
-            return 0
-
-        lax.fori_loop(0, height // tile, one, 0)
+        for tile in tiles(block):
+            grad = jnp.dot(act_t[tile[0], :], cot_all[:, tile[1]], preferred_element_type=jnp.float32)
+            new = (0.9 * m_in[tile].astype(jnp.float32) + grad).astype(jnp.bfloat16)
+            m_new[tile] = new
+            half[tile] = (w_in[tile].astype(jnp.float32) - 0.5 * new.astype(jnp.float32)).astype(jnp.bfloat16)
         e = len(blocks)
-        here = (pl.ds(r0, height), across)
+        here = (pl.ds(r0, height), pl.ds(c0, width))
         copy = pltpu.make_async_remote_copy(
             src_ref=half.at[here],
             dst_ref=other.at[here],
@@ -203,19 +208,12 @@
         outs.append(out)
         blocks.append(block)
 
-    for e, (r0, height, c0, width) in enumerate(blocks):
+    for e, block in enumerate(blocks):
+        r0, height, c0, width = block
         reps[e].wait_recv()
-        across = pl.ds(c0, width)
-
-        def mean(t, _):
-            down = pl.ds(pl.multiple_of(r0 + t * tile, tile), tile)
-            avg[down, across] = (
-                0.5 * (half[down, across].astype(jnp.float32) + other[down, across].astype(jnp.float32))
-            ).astype(jnp.bfloat16)
-            return 0
-
-        lax.fori_loop(0, height // tile, mean, 0)
-        here = (pl.ds(r0, height), across)
+        for tile in tiles(block):
+            avg[tile] = (0.5 * (half[tile].astype(jnp.float32) + other[tile].astype(jnp.float32))).astype(jnp.bfloat16)
+        here = (pl.ds(r0, height), pl.ds(c0, width))
         out = pltpu.make_async_copy(avg.at[here], avg_out.at[here], avg_sem.at[e])
         out.start()
         outs.append(out)
@@ -252,6 +250,7 @@
         out_specs=(anywhere, anywhere),
         scratch_shapes=[
             pltpu.VMEM((n_shard * tok, rows), jnp.bfloat16),
+            pltpu.VMEM((rows, n_shard * tok), jnp.bfloat16),
             pltpu.VMEM((n_shard * tok, cols), jnp.bfloat16),
             *[whole] * 6,
             dma((4,)),

time: 73.4 us -> 73 us (level)
  Pallas kernels: 69 us -> 68.2 us
    pallas_call x1, Pallas kernels: 69 us -> 68.2 us  [fused(): pl.pallas_call(functools.partial(kernel, n_rep, n_shard, 1 << level), out...]
where the time goes in v1:
time: 73 us; the launch traced here: 72.4 us
  Pallas kernels  68.2 us (93%)
  local copies, waits for them, and re-layouts  2.46 us (3%)
  between operations  1.3 us (2%)
    pallas_call x1, Pallas kernels, fused(): pl.pallas_call(functools.partial(kernel, n_rep, n_shard, 1 << level), out...  68.2 us
    unnamed x2, local copies, waits for them, and re-layouts  2.46 us

profile of v1, /device:TPU:0, one launch (start us, length us, event | category | flops | bytes accessed | tf_op | source)
XLA Modules:
  0.0 72.4 jit_solution(4479331494992478953)
XLA Ops:
  1.3 68.6 %conditional.1 = ((bf16[1024,896]{1,0:T(8,128)(2,1)S(1)}, bf16[1024,896]{1,0:T(8,128)(2,1)S(1)})) conditional(s32[]{:T(128)} %clamp.3, (bf16[128,4096]{1,0:T(8,128)(2,1)}, bf16[128,896]{1,0:T(8,128)(2,1)}, bf16[1024,896]{1,0:T(8,128)(2,1)}, bf16[1024,896]{1,0:T(8,128)(2,1)}) %tuple.41, (bf16[128,4096]{1,0:T(8,128)(2,1)}, ...), branch_computations={%region_0.1_spmd, %region_1.2_spmd, %region_2.3_spmd} | conditional | flops 939524096 | bytes 9175048 | solution.py:279
  1.5 68.2 %branch_2_fun.1 = (bf16[1024,896]{1,0:T(8,128)(2,1)S(1)}, bf16[1024,896]{1,0:T(8,128)(2,1)S(1)}) custom-call(bf16[128,4096]{1,0:T(8,128)(2,1)} %get-tuple-element.44.act, bf16[128,896]{1,0:T(8,128)(2,1)} %get-tuple-element.45.cot, bf16[1024,896]{1,0:T(8,128)(2,1)} %get-tuple-element.46.weight, bf16[1024,896]{1,0:T(8,128)(2,1)} %get-tuple-element.47.momentum), custom_call_target="tpu_custom_call" | custom-call | flops 939524096 | bytes 9175040 | tf_op jit(solution)/shard_map/cond/branch_2_fun/pallas_call | solution.py:246
  69.9 1.2 %copy.16 = bf16[1,1024,896]{2,1,0:T(8,128)(2,1)} copy(bf16[1,1024,896]{2,1,0:T(8,128)(2,1)S(1)} %bitcast.11) | data formatting | bytes 3670016
  71.1 1.2 %copy.17 = bf16[1,1024,896]{2,1,0:T(8,128)(2,1)} copy(bf16[1,1024,896]{2,1,0:T(8,128)(2,1)S(1)} %bitcast.12) | data formatting | bytes 3670016
